TPU v7x, 256 devices: a whole 4x4x8 slice. The times are simulated.
256 devices in a mesh: grp: 8 (over x_hi, y), dev: 32 (over x_lo, z, core).
Axes of the slice: x: 4 (x_hi: 2, x_lo: 2; x = x_hi * 2 + x_lo), y: 4, z: 8, core: 2. Of those that a mesh axis runs over, the one named last changes fastest.
Arguments:
- state: float32 [8, 32, 524288], P('grp', 'dev'), may hold values from -6 to 6
- angles: float32 [2, 27], replicated, may hold values from -3.140625 to 3.140625
Outputs:
- evolved: float32 [8, 32, 524288], P('grp', 'dev')
All inputs are finite; a program needn't handle non-finite values.
Results may differ from a plain program's by a relative error of at most 0.00014.
Values sent between devices are 32-bit elements; how exact they have to be, the bound alone decides.
A program may use at most 192 MiB of HBM per device.

v0:
```python
import jax
import jax.numpy as jnp
from jax import lax
from jax.sharding import PartitionSpec as P

LAYERS = 2


HIGH = lax.Precision.HIGHEST


def ladder(values, nbits):
    total = jnp.zeros_like(values)
    for j in range(nbits - 1):
        total = total + (values >> j & values >> j + 1 & 1)
    return total % 2


def joined_gate(slot_angles):
    index = jnp.arange(128, dtype=jnp.int32)
    rows = index[:, None]
    cols = index[None, :]
    matrix = jnp.ones((128, 128), slot_angles.dtype)
    for j in range(7):
        cosine = jnp.cos(0.5 * slot_angles[j])
        sine = jnp.sin(0.5 * slot_angles[j])
        row_bit = rows >> j & 1
        col_bit = cols >> j & 1
        entry = jnp.where(row_bit == col_bit, cosine, jnp.where(row_bit == 1, sine, -sine))
        matrix = matrix * entry
    return matrix


def gate_plan(local_bits, dev_bits, grp_bits):
    claimed_qubits = []

    def claim(wanted):
        chosen_slots = []
        for qubit_id in wanted:
            if qubit_id in claimed_qubits:
                chosen_slots.append(-1)
            else:
                claimed_qubits.append(qubit_id)
                chosen_slots.append(qubit_id)
        return chosen_slots

    grp_slots = claim(
        list(range(7 - grp_bits)) + [local_bits + dev_bits + j for j in range(grp_bits)]
    )
    dev_slots = claim(
        [local_bits - 7 + j for j in range(7 - dev_bits)]
        + [local_bits + j for j in range(dev_bits)]
    )
    offsets = list(range(0, local_bits - 6, 7))
    offsets.append(local_bits - 7)
    windows = []
    for offset in offsets:
        slot_list = claim(list(range(offset, offset + 7)))
        windows.append((offset, slot_list))
    return (windows, dev_slots, grp_slots)


def slot_gate(angles, layer, slot_list):
    picked = [angles[layer, k] if k >= 0 else jnp.zeros((), angles.dtype) for k in slot_list]
    return joined_gate(jnp.stack(picked))


def apply_lowest(flat, gate):
    return jnp.dot(flat.reshape(-1, 128), gate.T, precision=HIGH).reshape(-1)


def apply_highest(flat, gate):
    return jnp.dot(gate, flat.reshape(128, -1), precision=HIGH).reshape(-1)


def apply_window(flat, gate, offset):
    if offset == 0:
        return apply_lowest(flat, gate)
    shaped = flat.reshape(-1, 128, 2**offset)
    return jnp.einsum("ab,ibk->iak", gate, shaped, precision=HIGH).reshape(-1)


def remap_dev(flat, n_dev):
    moved = lax.all_to_all(flat.reshape(n_dev, -1), "dev", split_axis=0, concat_axis=0, tiled=True)
    return moved.reshape(-1)


def remap_grp(flat, n_grp):
    shaped = flat.reshape(-1, n_grp, 128 // n_grp)
    return lax.all_to_all(shaped, "grp", split_axis=1, concat_axis=1, tiled=True).reshape(-1)


def shards(state, angles):
    n_grp = lax.axis_size("grp")
    n_dev = lax.axis_size("dev")
    grp_bits = n_grp.bit_length() - 1
    dev_bits = n_dev.bit_length() - 1
    amp = state.shape[2]
    local_bits = amp.bit_length() - 1
    upper = amp // 128
    windows, dev_slots, grp_slots = gate_plan(local_bits, dev_bits, grp_bits)
    device = lax.axis_index("grp") * n_dev + lax.axis_index("dev")
    high_idx = jnp.arange(upper, dtype=jnp.int32)
    low_idx = jnp.arange(128, dtype=jnp.int32)
    parity = ladder(high_idx, local_bits - 7)[:, None] + ladder(low_idx, 7)[None, :]
    parity = parity + (high_idx & 1)[:, None] * (low_idx >> 6 & 1)[None, :]
    top_bit = high_idx >> local_bits - 8 & 1
    parity = parity + ladder(device, dev_bits + grp_bits) + (top_bit * (device & 1))[:, None]
    signs = (1 - 2 * (parity % 2)).astype(state.dtype).reshape(-1)
    x = state.reshape(-1)
    for layer in range(LAYERS):
        for offset, slot_list in windows:
            x = apply_window(x, slot_gate(angles, layer, slot_list), offset)
        dev_gate = slot_gate(angles, layer, dev_slots)
        grp_gate = slot_gate(angles, layer, grp_slots)
        x = remap_dev(x, n_dev)
        x = apply_highest(x, dev_gate)
        x = remap_dev(x, n_dev)
        x = remap_grp(x, n_grp)
        x = apply_lowest(x, grp_gate)
        x = remap_grp(x, n_grp)
        x = x * signs
    return x.reshape(1, 1, amp)


def solution(mesh):
    placed = (P("grp", "dev", None), P())
    return jax.shard_map(
        shards, mesh=mesh, in_specs=placed, out_specs=P("grp", "dev", None), check_vma=False
    )
```

profile of v0, /device:TPU:56, one launch (start us, length us, event | category | flops | bytes accessed | tf_op | source)
XLA Modules:
  0.0 535.4 jit_solution(12886919519664553725)
XLA Ops:
  35.6 10.2 %all-to-all-start = ((f32[32,1,16384]{2,1,0:T(1,128)}), f32[32,1,16384]{2,1,0:T(1,128)S(1)}, u32[]{:S(2)}, u32[]{:S(2)}) async-start(f32[32,1,16384]{2,1,0:T(1,128)} %all_to_all.48), calls=%async_computation | async-start | bytes 4194304 | tf_op jit(solution)/shard_map/all_to_all | solution.py:84
  51.2 45.9 %all-to-all-done = f32[32,1,16384]{2,1,0:T(1,128)S(1)} async-done(((f32[32,1,16384]{2,1,0:T(1,128)}), f32[32,1,16384]{2,1,0:T(1,128)S(1)}, u32[]{:S(2)}, u32[]{:S(2)}) %all-to-all-start) | async-done | bytes 2097184 | tf_op jit(solution)/shard_map/all_to_all | solution.py:84
  97.1 7.0 %reduce = f32[32,16384]{1,0:T(8,128)} reduce(f32[32,1,16384]{2,1,0:T(1,128)S(1)} %all-to-all-done, f32[]{:T(128)} %constant.188.clone.1), dimensions={1}, to_apply=%all_to_all.37.reduce_sub_computation | reduce | bytes 4194308 | tf_op jit(solution)/shard_map/all_to_all | solution.py:84
  113.2 55.0 %all_to_all.60 = f32[32,1,16384]{2,1,0:T(1,128)} all-to-all(f32[32,1,16384]{2,1,0:T(1,128)S(1)} %all_to_all.49), channel_id=1, replica_groups=mesh['grp'=8,'dev'=32] {'dev'}, dimensions={0} | all-to-all | bytes 4194304 | tf_op jit(solution)/shard_map/all_to_all | solution.py:84
  168.2 6.7 %reduce.1 = f32[32,16384]{1,0:T(8,128)S(1)} reduce(f32[32,1,16384]{2,1,0:T(1,128)} %all_to_all.60, f32[]{:T(128)} %constant.188.clone.1), dimensions={1}, to_apply=%all_to_all.39.reduce_sub_computation | reduce | bytes 4194308 | tf_op jit(solution)/shard_map/all_to_all | solution.py:84
  174.9 8.2 %reshape_reshape.36 = f32[4096,8,16]{2,1,0:T(8,128)} reshape(f32[32,16384]{1,0:T(8,128)S(1)} %reduce.1) | data formatting | bytes 4194304 | tf_op jit(solution)/shard_map/reshape;reshape | solution.py:89
  183.2 10.6 %copy.19 = f32[4096,8,16]{0,2,1:T(8,128)} copy(f32[4096,8,16]{2,1,0:T(8,128)} %reshape_reshape.36) | data formatting | bytes 4194304 | tf_op jit(solution)/shard_map/reshape;reshape | solution.py:89
  193.7 6.9 %all-to-all-start.2 = ((f32[4096,8,16]{0,2,1:T(8,128)}), f32[4096,8,16]{0,2,1:T(8,128)S(1)}, u32[]{:S(2)}, u32[]{:S(2)}) async-start(f32[4096,8,16]{0,2,1:T(8,128)} %copy.19), calls=%async_computation.2 | async-start | bytes 4194304 | tf_op jit(solution)/shard_map/all_to_all | solution.py:90
  206.1 19.6 %all-to-all-done.2 = f32[4096,8,16]{0,2,1:T(8,128)S(1)} async-done(((f32[4096,8,16]{0,2,1:T(8,128)}), f32[4096,8,16]{0,2,1:T(8,128)S(1)}, u32[]{:S(2)}, u32[]{:S(2)}) %all-to-all-start.2) | async-done | bytes 2097184 | tf_op jit(solution)/shard_map/all_to_all | solution.py:90
  229.2 5.6 %all-to-all-start.3 = ((f32[4096,8,16]{0,2,1:T(8,128)}), f32[4096,8,16]{0,2,1:T(8,128)S(1)}, u32[]{:S(2)}, u32[]{:S(2)}) async-start(f32[4096,8,16]{0,2,1:T(8,128)} %fusion.40), calls=%async_computation.3 | async-start | bytes 4194304 | tf_op jit(solution)/shard_map/all_to_all | solution.py:90
  244.6 16.5 %all-to-all-done.3 = f32[4096,8,16]{0,2,1:T(8,128)S(1)} async-done(((f32[4096,8,16]{0,2,1:T(8,128)}), f32[4096,8,16]{0,2,1:T(8,128)S(1)}, u32[]{:S(2)}, u32[]{:S(2)}) %all-to-all-start.3) | async-done | bytes 2097184 | tf_op jit(solution)/shard_map/all_to_all | solution.py:90
  294.2 46.1 %all-to-all-done.4 = f32[32,1,16384]{2,1,0:T(1,128)S(1)} async-done(((f32[32,1,16384]{2,1,0:T(1,128)}), f32[32,1,16384]{2,1,0:T(1,128)S(1)}, u32[]{:S(2)}, u32[]{:S(2)}) %all-to-all-start.4) | async-done | bytes 2097184 | tf_op jit(solution)/shard_map/all_to_all | solution.py:84
  340.3 7.0 %reduce.2 = f32[32,16384]{1,0:T(8,128)} reduce(f32[32,1,16384]{2,1,0:T(1,128)S(1)} %all-to-all-done.4, f32[]{:T(128)} %constant.188.clone.1), dimensions={1}, to_apply=%all_to_all.43.reduce_sub_computation | reduce | bytes 4194308 | tf_op jit(solution)/shard_map/all_to_all | solution.py:84
  356.4 55.0 %all_to_all.61 = f32[32,1,16384]{2,1,0:T(1,128)} all-to-all(f32[32,1,16384]{2,1,0:T(1,128)S(1)} %all_to_all.51), channel_id=1, replica_groups=mesh['grp'=8,'dev'=32] {'dev'}, dimensions={0} | all-to-all | bytes 4194304 | tf_op jit(solution)/shard_map/all_to_all | solution.py:84
  411.4 6.7 %reduce.3 = f32[32,16384]{1,0:T(8,128)S(1)} reduce(f32[32,1,16384]{2,1,0:T(1,128)} %all_to_all.61, f32[]{:T(128)} %constant.188.clone.1), dimensions={1}, to_apply=%all_to_all.45.reduce_sub_computation | reduce | bytes 4194308 | tf_op jit(solution)/shard_map/all_to_all | solution.py:84
  418.1 8.2 %reshape_reshape.39 = f32[4096,8,16]{2,1,0:T(8,128)} reshape(f32[32,16384]{1,0:T(8,128)S(1)} %reduce.3) | data formatting | bytes 4194304 | tf_op jit(solution)/shard_map/reshape;reshape | solution.py:89
  426.3 10.6 %copy.27 = f32[4096,8,16]{0,2,1:T(8,128)} copy(f32[4096,8,16]{2,1,0:T(8,128)} %reshape_reshape.39) | data formatting | bytes 4194304 | tf_op jit(solution)/shard_map/reshape;reshape | solution.py:89
  436.9 5.6 %all-to-all-start.6 = ((f32[4096,8,16]{0,2,1:T(8,128)}), f32[4096,8,16]{0,2,1:T(8,128)S(1)}, u32[]{:S(2)}, u32[]{:S(2)}) async-start(f32[4096,8,16]{0,2,1:T(8,128)} %copy.27), calls=%async_computation.6 | async-start | bytes 4194304 | tf_op jit(solution)/shard_map/all_to_all | solution.py:90
  448.0 19.6 %all-to-all-done.6 = f32[4096,8,16]{0,2,1:T(8,128)S(1)} async-done(((f32[4096,8,16]{0,2,1:T(8,128)}), f32[4096,8,16]{0,2,1:T(8,128)S(1)}, u32[]{:S(2)}, u32[]{:S(2)}) %all-to-all-start.6) | async-done | bytes 2097184 | tf_op jit(solution)/shard_map/all_to_all | solution.py:90
  471.1 5.6 %all-to-all-start.7 = ((f32[4096,8,16]{0,2,1:T(8,128)}), f32[4096,8,16]{0,2,1:T(8,128)S(1)}, u32[]{:S(2)}, u32[]{:S(2)}) async-start(f32[4096,8,16]{0,2,1:T(8,128)} %fusion.48), calls=%async_computation.7 | async-start | bytes 4194304 | tf_op jit(solution)/shard_map/all_to_all | solution.py:90
  481.3 21.7 %all-to-all-done.7 = f32[4096,8,16]{0,2,1:T(8,128)S(1)} async-done(((f32[4096,8,16]{0,2,1:T(8,128)}), f32[4096,8,16]{0,2,1:T(8,128)S(1)}, u32[]{:S(2)}, u32[]{:S(2)}) %all-to-all-start.7) | async-done | bytes 2097184 | tf_op jit(solution)/shard_map/all_to_all | solution.py:90
  503.0 8.8 %copy.29 = f32[4096,8,16]{2,1,0:T(8,128)} copy(f32[4096,8,16]{0,2,1:T(8,128)S(1)} %all-to-all-done.7) | data formatting | bytes 4194304 | tf_op jit(solution)/shard_map/all_to_all | solution.py:90
  511.8 13.1 %reshape.1091 = f32[1,1,524288]{2,1,0:T(1,128)} reshape(f32[4096,8,16]{2,1,0:T(8,128)} %copy.29) | data formatting | bytes 4194304 | tf_op jit(solution)/shard_map/reshape | solution.py:90
  524.9 10.3 %fusion.10 = f32[1,1,524288]{2,1,0:T(1,128)} fusion(f32[1,1,524288]{2,1,0:T(1,128)} %reshape.1091, s32[1,1,524288]{2,1,0:T(1,128)} %bitcast.159), kind=kLoop, calls=%fused_computation.17 | loop fusion | flops 7864320 | bytes 6291456 | tf_op jit(solution)/shard_map/mul | solution.py:122
  (78 shorter events, 82.2 us)
Async XLA Ops:
  0.0 17.2 %copy-start = (f32[1,1,524288]{2,1,0:T(1,128)S(1)}, f32[1,1,524288]{2,1,0:T(1,128)}, u32[]{:S(2)}) copy-start(f32[1,1,524288]{2,1,0:T(1,128)} %param.2) | copy-start | bytes 6291460
  35.6 61.6 %all-to-all-start = ((f32[32,1,16384]{2,1,0:T(1,128)}), f32[32,1,16384]{2,1,0:T(1,128)S(1)}, u32[]{:S(2)}, u32[]{:S(2)}) async-start(f32[32,1,16384]{2,1,0:T(1,128)} %all_to_all.48), calls=%async_computation | async-start | bytes 4194304 | tf_op jit(solution)/shard_map/all_to_all | solution.py:84
  193.7 31.9 %all-to-all-start.2 = ((f32[4096,8,16]{0,2,1:T(8,128)}), f32[4096,8,16]{0,2,1:T(8,128)S(1)}, u32[]{:S(2)}, u32[]{:S(2)}) async-start(f32[4096,8,16]{0,2,1:T(8,128)} %copy.19), calls=%async_computation.2 | async-start | bytes 4194304 | tf_op jit(solution)/shard_map/all_to_all | solution.py:90
  229.2 31.9 %all-to-all-start.3 = ((f32[4096,8,16]{0,2,1:T(8,128)}), f32[4096,8,16]{0,2,1:T(8,128)S(1)}, u32[]{:S(2)}, u32[]{:S(2)}) async-start(f32[4096,8,16]{0,2,1:T(8,128)} %fusion.40), calls=%async_computation.3 | async-start | bytes 4194304 | tf_op jit(solution)/shard_map/all_to_all | solution.py:90
  285.0 55.3 %all-to-all-start.4 = ((f32[32,1,16384]{2,1,0:T(1,128)}), f32[32,1,16384]{2,1,0:T(1,128)S(1)}, u32[]{:S(2)}, u32[]{:S(2)}) async-start(f32[32,1,16384]{2,1,0:T(1,128)} %all_to_all.50), calls=%async_computation.4 | async-start | bytes 4194304 | tf_op jit(solution)/shard_map/all_to_all | solution.py:84
  436.9 30.6 %all-to-all-start.6 = ((f32[4096,8,16]{0,2,1:T(8,128)}), f32[4096,8,16]{0,2,1:T(8,128)S(1)}, u32[]{:S(2)}, u32[]{:S(2)}) async-start(f32[4096,8,16]{0,2,1:T(8,128)} %copy.27), calls=%async_computation.6 | async-start | bytes 4194304 | tf_op jit(solution)/shard_map/all_to_all | solution.py:90
  471.1 31.9 %all-to-all-start.7 = ((f32[4096,8,16]{0,2,1:T(8,128)}), f32[4096,8,16]{0,2,1:T(8,128)S(1)}, u32[]{:S(2)}, u32[]{:S(2)}) async-start(f32[4096,8,16]{0,2,1:T(8,128)} %fusion.48), calls=%async_computation.7 | async-start | bytes 4194304 | tf_op jit(solution)/shard_map/all_to_all | solution.py:90
  524.9 10.3 %copy-start.1 = (f32[1,1,524288]{2,1,0:T(1,128)S(1)}, f32[1,1,524288]{2,1,0:T(1,128)}, u32[]{:S(2)}) copy-start(f32[1,1,524288]{2,1,0:T(1,128)} %param.2) | copy-start | bytes 6291460
where the time goes:
time: 545 us; the launch traced here: 535 us
  waiting for transfers between devices  169 us (31%)
  blocking collectives  110 us (20%)
  local copies, waits for them, and re-layouts  99 us (18%)
  other arithmetic  42.9 us (8%)
  between operations  42.7 us (8%)
  starting transfers between devices  37.7 us (7%)
  matrix products  33.8 us (6%)
    all_to_all x2, blocking collectives, remap_dev(): lax.all_to_all(flat.reshape(n_dev, -1), 'dev', split_axis=0, concat_axis=...  110 us
    all_to_all x2, waiting for transfers between devices, remap_dev(): lax.all_to_all(flat.reshape(n_dev, -1), 'dev', split_axis=0, concat_axis=...  92 us
    all_to_all x4, waiting for transfers between devices, remap_grp(): lax.all_to_all(shaped, 'grp', split_axis=1, concat_axis=1, tiled=True)  77.4 us
    another operation x4, local copies, waits for them, and re-layouts, remap_grp(): shaped = flat.reshape(-1, n_grp, 128 // n_grp)  37.6 us
    all_to_all x4, other arithmetic, remap_dev(): lax.all_to_all(flat.reshape(n_dev, -1), 'dev', split_axis=0, concat_axis=...  27.5 us
    all_to_all x4, starting transfers between devices, remap_grp(): lax.all_to_all(shaped, 'grp', split_axis=1, concat_axis=1, tiled=True)  23.6 us
    reshape x2, local copies, waits for them, and re-layouts, remap_grp(): lax.all_to_all(shaped, 'grp', split_axis=1, concat_axis=1, tiled=True)  15.1 us
    all_to_all x4, local copies, waits for them, and re-layouts, remap_dev(): lax.all_to_all(flat.reshape(n_dev, -1), 'dev', split_axis=0, concat_axis=...  14.9 us
  transfers between devices with their start and end apart: 6, of which 6 were waited for; matrix products, arithmetic and copies ran while one was open for 1% of the time, Pallas kernels for 0%

commit v1 on v0

v1 whole, which is shorter than its diff:
```python
import jax
import jax.numpy as jnp
from jax import lax
from jax.experimental import pallas as pl
from jax.experimental.pallas import tpu as pltpu
from jax.sharding import PartitionSpec as P

MESH = pl.DeviceIdType.MESH
F32, BF16 = jnp.float32, jnp.bfloat16
W_QUBITS = (19, 23, 24, 25, 26)
BW_QUBITS = (11, 12, 13, 14, 15)
ROW_QUBITS = (7, 8, 9) + W_QUBITS
COL_QUBITS = (0, 1, 2, 3, 4, 5, 6, 20)
QUARTERS = 4


def rotate(tiles, bit, gate):
    cosine, sine = gate
    out = list(tiles)
    for i in range(len(tiles)):
        if not i >> bit & 1:
            j = i | 1 << bit
            out[i] = cosine * tiles[i] - sine * tiles[j]
            out[j] = sine * tiles[i] + cosine * tiles[j]
    return out


def ladder(values, nbits):
    total = values & values >> 1
    parity = total & 1
    for j in range(1, nbits - 1):
        parity = parity + (total >> j & 1)
    return parity


def signs(parity):
    return (1 - 2 * (parity & 1)).astype(F32)


def split(value):
    high = value.astype(BF16)
    return high, (value - high.astype(F32)).astype(BF16)


def dot3(a, b):
    return (
        jnp.dot(a[0], b[0], preferred_element_type=F32)
        + jnp.dot(a[0], b[1], preferred_element_type=F32)
        + jnp.dot(a[1], b[0], preferred_element_type=F32)
    )


def kernel(
    state, angles, out,
    x, p_buf, q_buf, q2, w_buf, m_buf, v_buf, v2, t_buf, o_buf, ys, cz, gate_hi, gate_lo,
    load_sem, store_sem, fz_s, fz_r, fw_s, fw_r, bw_s, bw_r, bz_s, bz_r, last_s, last_r,
):
    grp, dev = lax.axis_index("grp"), lax.axis_index("dev")
    core, my_z, x_lo = lax.rem(dev, 2), lax.rem(lax.div(dev, 2), 8), lax.div(dev, 16)
    my_w = core + 2 * x_lo + 4 * grp
    my_p, my_h = lax.rem(my_z, 2), lax.div(my_z, 2)

    def z_device(z):
        return (grp, 16 * x_lo + 2 * z + core)

    def w_device(w):
        return (lax.div(w, 4), 16 * lax.rem(lax.div(w, 2), 2) + 2 * my_z + lax.rem(w, 2))

    def other_w(k):
        return lax.rem(my_w + k, 32)

    def load(i):
        part = pl.ds(8 * i, 8)
        return pltpu.make_async_copy(state.at[:, part], x.at[:, part], load_sem.at[i])

    def store(i):
        part = pl.ds(8 * i, 8)
        return pltpu.make_async_copy(o_buf.at[:, part], out.at[:, part], store_sem.at[i])

    for i in range(QUARTERS):
        load(i).start()
    barrier = pltpu.get_barrier_semaphore()

    @pl.loop(1, 8)
    def _(k):
        pl.semaphore_signal(barrier, inc=1, device_id=z_device(lax.rem(my_z + k, 8)), device_id_type=MESH)

    @pl.loop(1, 32)
    def _(k):
        pl.semaphore_signal(barrier, inc=1, device_id=w_device(other_w(k)), device_id_type=MESH)

    half = 0.5 * angles[...]
    cosines, sines = jnp.cos(half), jnp.sin(half)

    def gate(layer, qubit, shape=(8, 128)):
        at = (slice(layer, layer + 1), slice(qubit, qubit + 1))
        return jnp.broadcast_to(cosines[at], shape), jnp.broadcast_to(sines[at], shape)

    first = [gate(0, q) for q in (10, 16, 17, 18)]
    for i in range(QUARTERS):
        load(i).wait()

        @pl.loop(8 * i, 8 * i + 8)
        def _(bw):
            tiles = [x[j >> 1, bw, j & 1] for j in range(16)]
            for bit in range(4):
                tiles = rotate(tiles, bit, first[bit])
            for j in range(16):
                z = j >> 1
                p_buf[j & 1, z & 1, z >> 1, bw] = tiles[j]

    pl.semaphore_wait(barrier, 38)

    def send_z(source, target, c, g, send_sem, recv_sem):
        def one(h, p):
            pltpu.make_async_remote_copy(
                src_ref=source.at[c, p, h], dst_ref=target.at[c, my_p, my_h],
                send_sem=send_sem.at[c, g], recv_sem=recv_sem.at[c, g],
                device_id=z_device(2 * h + p), device_id_type=MESH,
            ).start()

        if g == 0:
            @pl.loop(0, 4)
            def _(k):
                one(lax.rem(my_h + k, 4), 1 - my_p)
        else:
            @pl.loop(1, 4)
            def _(k):
                one(lax.rem(my_h + k, 4), my_p)

    def wait_z(buffer, c, g, sem):
        part = buffer.at[c, 1 - my_p] if g == 0 else buffer.at[c, my_p, pl.ds(0, 3)]
        pltpu.make_async_copy(part, part, sem.at[c, g]).wait()

    def send_w(source, target, c, g, send_sem, recv_sem):
        p = 1 - my_p if g == 0 else my_p

        @pl.loop(1, 32)
        def _(k):
            w = other_w(k)
            pltpu.make_async_remote_copy(
                src_ref=source.at[c, w, p], dst_ref=target.at[c, my_w, p],
                send_sem=send_sem.at[c, g], recv_sem=recv_sem.at[c, g],
                device_id=w_device(w), device_id_type=MESH,
            ).start()

        target[c, my_w, p] = source[c, my_w, p]

    def wait_w(buffer, c, g, sem):
        part = buffer.at[c, pl.ds(0, 31), 0]
        pltpu.make_async_copy(part, part, sem.at[c, g]).wait()

    send_z(p_buf, q_buf, 0, 0, fz_s, fz_r)
    send_z(p_buf, q_buf, 0, 1, fz_s, fz_r)

    for c in range(2):
        q_buf[c, my_p, my_h] = p_buf[c, my_p, my_h]

    square = (256, 256)
    rows = lax.broadcasted_iota(jnp.int32, square, 0)
    cols = lax.broadcasted_iota(jnp.int32, square, 1)
    for layer in range(2):
        for side, qubits in enumerate((ROW_QUBITS, COL_QUBITS)):
            matrix = None
            for j, q in enumerate(qubits):
                cosine, sine = gate(layer, q, square)
                to, of = (rows, cols) if side == 0 else (cols, rows)
                a, b = to >> j & 1, of >> j & 1
                entry = jnp.where(a == b, cosine, jnp.where(a == 1, sine, -sine))
                matrix = entry if matrix is None else matrix * entry
            gate_hi[layer, side], gate_lo[layer, side] = split(matrix)

    w_row, p_col = rows >> 3, cols >> 7
    fixed = ladder(my_w, 5) + ladder(my_z, 3) + (my_w >> 4 & my_z & 1)
    cross = (
        ladder(cols & 127, 7) + (cols >> 6 & rows & 1) + ladder(rows & 7, 3) + (my_z >> 2 & w_row & 1)
        + (w_row & p_col & 1) + ladder(w_row >> 1, 4) + fixed
    )
    for h in range(4):
        with_h = cross + (p_col & h & 1) + (h >> 1 & w_row >> 1 & 1) + (h & h >> 1 & 1)
        cz[0, h] = signs(with_h)
        cz[1, h] = signs(with_h + (rows >> 2 & 1) + (my_w & 1))

    def rotate_bw(source, target, c, p, layer, forward):
        gates = [gate(layer, q) for q in BW_QUBITS]

        @pl.loop(0, 4)
        def _(h):
            tiles = [source[c, p, h, w] if forward else source[c, w, p, h] for w in range(32)]
            for bit in range(5):
                tiles = rotate(tiles, bit, gates[bit])
            for w in range(32):
                if forward:
                    target[c, w, p, h] = tiles[w]
                else:
                    target[c, p, h, w] = tiles[w]

    h_gates = [[gate(layer, q, (8, 256)) for q in (21, 22)] for layer in range(2)]

    def middle(c):
        def both_sides(layer, block):
            left = (gate_hi[layer, 0], gate_lo[layer, 0])
            right = (gate_hi[layer, 1], gate_lo[layer, 1])
            return dot3(split(dot3(left, split(block))), right)

        @pl.loop(0, 4)
        def _(h):
            block = jnp.concatenate([w_buf[c, :, p, h].reshape(256, 128) for p in range(2)], axis=1)
            ys[h] = both_sides(0, block)

        @pl.loop(0, 32)
        def _(r):
            part = pl.ds(pl.multiple_of(8 * r, 8), 8)
            tiles = [ys[h, part] for h in range(4)]
            for layer in range(2):
                for bit in range(2):
                    tiles = rotate(tiles, bit, h_gates[layer][bit])
                if layer == 0:
                    tiles = [tiles[h] * cz[c, h, part] for h in range(4)]
            for h in range(4):
                ys[h, part] = tiles[h]

        @pl.loop(0, 4)
        def _(h):
            block = both_sides(1, ys[h])
            for p in range(2):
                m_buf[c, :, p, h] = block[:, 128 * p:128 * p + 128].reshape(32, 8, 128)

    def forward_z(c, g):
        wait_z(q_buf, c, g, fz_r)
        if c == 0:
            send_z(p_buf, q_buf, 1, g, fz_s, fz_r)
        rotate_bw(q_buf, q2, c, 1 - my_p if g == 0 else my_p, 0, True)
        send_w(q2, w_buf, c, g, fw_s, fw_r)

    def forward_w(c):
        for g in range(2):
            wait_w(w_buf, c, g, fw_r)
        middle(c)
        for g in range(2):
            send_w(m_buf, v_buf, c, g, bw_s, bw_r)

    def backward_w(c, g):
        wait_w(v_buf, c, g, bw_r)
        rotate_bw(v_buf, v2, c, 1 - my_p if g == 0 else my_p, 1, False)
        if c == 0 or g == 0:
            send_z(v2, t_buf, c, g, bz_s, bz_r)
        else:
            for i in range(QUARTERS):
                part = pl.ds(8 * i, 8)

                @pl.loop(1, 4)
                def _(k):
                    h = lax.rem(my_h + k, 4)
                    pltpu.make_async_remote_copy(
                        src_ref=v2.at[c, my_p, h, part], dst_ref=t_buf.at[c, my_p, my_h, part],
                        send_sem=last_s.at[i], recv_sem=last_r.at[i],
                        device_id=z_device(2 * h + my_p), device_id_type=MESH,
                    ).start()
        if g == 1:
            t_buf[c, my_p, my_h] = v2[c, my_p, my_h]

    forward_z(0, 0)
    forward_z(0, 1)
    forward_w(0)
    forward_z(1, 0)
    backward_w(0, 0)
    forward_z(1, 1)
    backward_w(0, 1)
    forward_w(1)
    backward_w(1, 0)
    backward_w(1, 1)

    second = [gate(1, q) for q in (10, 16, 17, 18)]
    sub = lax.broadcasted_iota(jnp.int32, (8, 128), 0)
    lane = lax.broadcasted_iota(jnp.int32, (8, 128), 1)
    base = ladder(lane, 7) + (lane >> 6 & sub & 1) + ladder(sub, 3)
    base = base + ladder(dev, 5) + ladder(grp, 3) + (dev >> 4 & grp & 1)
    tile_signs = [signs(base + c * (sub >> 2 & 1)) for c in range(2)]
    for c, g in ((0, 0), (0, 1), (1, 0)):
        wait_z(t_buf, c, g, bz_r)
    for i in range(QUARTERS):
        part = t_buf.at[1, 0, pl.ds(0, 3), pl.ds(8 * i, 8)]
        pltpu.make_async_copy(part, part, last_r.at[i]).wait()

        @pl.loop(8 * i, 8 * i + 8)
        def _(bw):
            tiles = [t_buf[j & 1, j >> 1 & 1, j >> 2, bw] for j in range(16)]
            for bit in range(4):
                tiles = rotate(tiles, bit, second[bit])
            for j in range(16):
                c, z = j & 1, j >> 1
                parity = ladder(bw, 5) + (c & bw & 1) + (bw >> 4 & z & 1) + (z >> 2 & core & 1)
                parity = parity + (z & z >> 1 & 1) + (z >> 1 & z >> 2 & 1)
                o_buf[z, bw, c] = tiles[j] * (tile_signs[c] * signs(parity))

        store(i).start()

    for c in range(2):
        for g in range(2):
            wait_z(p_buf, c, g, fz_s)
            wait_w(q2, c, g, fw_s)
            wait_w(m_buf, c, g, bw_s)
            if c == 0 or g == 0:
                wait_z(v2, c, g, bz_s)
    for i in range(QUARTERS):
        part = v2.at[1, 0, pl.ds(0, 3), pl.ds(8 * i, 8)]
        pltpu.make_async_copy(part, part, last_s.at[i]).wait()
        store(i).wait()


def shards(state, angles):
    view = (8, 32, 2, 8, 128)
    by_z = (2, 2, 4, 32, 8, 128)
    by_w = (2, 32, 2, 4, 8, 128)
    pairs = pltpu.SemaphoreType.DMA((2, 2))
    quarters = pltpu.SemaphoreType.DMA((QUARTERS,))
    out = pl.pallas_call(
        kernel,
        out_shape=jax.ShapeDtypeStruct(view, F32),
        in_specs=[pl.BlockSpec(memory_space=pl.ANY), pl.BlockSpec(memory_space=pltpu.VMEM)],
        out_specs=pl.BlockSpec(memory_space=pl.ANY),
        scratch_shapes=[
            pltpu.VMEM(view, F32),
            pltpu.VMEM(by_z, F32), pltpu.VMEM(by_z, F32),
            pltpu.VMEM(by_w, F32), pltpu.VMEM(by_w, F32), pltpu.VMEM(by_w, F32), pltpu.VMEM(by_w, F32),
            pltpu.VMEM(by_z, F32), pltpu.VMEM(by_z, F32),
            pltpu.VMEM(view, F32),
            pltpu.VMEM((4, 256, 256), F32),
            pltpu.VMEM((2, 4, 256, 256), F32),
            pltpu.VMEM((2, 2, 256, 256), BF16), pltpu.VMEM((2, 2, 256, 256), BF16),
            quarters, quarters,
            pairs, pairs, pairs, pairs, pairs, pairs, pairs, pairs,
            quarters, quarters,
        ],
        compiler_params=pltpu.CompilerParams(
            collective_id=0, has_side_effects=True, vmem_limit_bytes=48 * 2**20
        ),
    )(state.reshape(view), angles)
    return out.reshape(state.shape)


def solution(mesh):
    placed = (P("grp", "dev", None), P())
    return jax.shard_map(
        shards, mesh=mesh, in_specs=placed, out_specs=P("grp", "dev", None), check_vma=False
    )
```

time: 545 us -> 124 us (0.23)
  the two profiles are of different devices: /device:TPU:56 before, /device:TPU:1 now
where the time goes in v1:
time: 124 us
  Pallas kernels  121 us (98%)
  local copies, waits for them, and re-layouts  3.59 us (3%)
    pallas_call x1, Pallas kernels, shards(): pl.pallas_call(kernel, out_shape=jax.ShapeDtypeStruct(view, F32), in_spec...  121 us
    unnamed x5, local copies, waits for them, and re-layouts  3.59 us

profile of v1, /device:TPU:1, one launch (start us, length us, event | category | flops | bytes accessed | tf_op | source)
XLA Modules:
  0.0 124.1 jit_solution(15001388652944910715)
XLA Ops:
  0.0 0.0 copy-start
  0.0 1.6 %copy-done = f32[1,1,524288]{2,1,0:T(1,128)S(1)} copy-done((f32[1,1,524288]{2,1,0:T(1,128)S(1)}, f32[1,1,524288]{2,1,0:T(1,128)}, u32[]{:S(2)}) %copy-start) | copy-done | bytes 2097176
  1.6 0.0 copy-start.1
  1.6 0.7 copy-done.1
  2.3 120.5 %shard_map.28 = f32[8,32,2,8,128]{4,3,2,1,0:T(8,128)S(1)} custom-call(f32[8,32,2,8,128]{4,3,2,1,0:T(8,128)S(1)} %bitcast.3, f32[2,27]{1,0:T(2,128)S(1)} %copy-done.1), custom_call_target="tpu_custom_call" | custom-call | tf_op jit(solution)/shard_map/pallas_call | solution.py:318
  122.8 1.3 %copy.4 = f32[1,1,524288]{2,1,0:T(1,128)} copy(f32[1,1,524288]{2,1,0:T(1,128)S(1)} %bitcast.2) | data formatting | bytes 4194304
Async XLA Ops:
  0.0 1.6 %copy-start = (f32[1,1,524288]{2,1,0:T(1,128)S(1)}, f32[1,1,524288]{2,1,0:T(1,128)}, u32[]{:S(2)}) copy-start(f32[1,1,524288]{2,1,0:T(1,128)} %param.2) | copy-start | bytes 6291460
  1.6 0.7 copy-start.1

commit v2 on v1

--- a/solution.py
+++ b/solution.py
@@ -52,8 +52,8 @@
 
 def kernel(
     state, angles, out,
-    x, p_buf, q_buf, q2, w_buf, m_buf, v_buf, v2, t_buf, o_buf, ys, cz, gate_hi, gate_lo,
-    load_sem, store_sem, fz_s, fz_r, fw_s, fw_r, bw_s, bw_r, bz_s, bz_r, last_s, last_r,
+    x, turns, p_buf, q_buf, w_buf, m_buf, v_buf, t_buf, ys, cz, gate_left, gate_right,
+    load_sem, turns_sem, fz_s, fz_r, fw_s, fw_r, bw_s, bw_r, bz_s, bz_r, last_s, last_r,
 ):
     grp, dev = lax.axis_index("grp"), lax.axis_index("dev")
     core, my_z, x_lo = lax.rem(dev, 2), lax.rem(lax.div(dev, 2), 8), lax.div(dev, 16)
@@ -73,10 +73,8 @@
         part = pl.ds(8 * i, 8)
         return pltpu.make_async_copy(state.at[:, part], x.at[:, part], load_sem.at[i])
 
-    def store(i):
-        part = pl.ds(8 * i, 8)
-        return pltpu.make_async_copy(o_buf.at[:, part], out.at[:, part], store_sem.at[i])
-
+    load_turns = pltpu.make_async_copy(angles, turns, turns_sem)
+    load_turns.start()
     for i in range(QUARTERS):
         load(i).start()
     barrier = pltpu.get_barrier_semaphore()
@@ -89,7 +87,8 @@
     def _(k):
         pl.semaphore_signal(barrier, inc=1, device_id=w_device(other_w(k)), device_id_type=MESH)
 
-    half = 0.5 * angles[...]
+    load_turns.wait()
+    half = 0.5 * turns[...]
     cosines, sines = jnp.cos(half), jnp.sin(half)
 
     def gate(layer, qubit, shape=(8, 128)):
@@ -139,22 +138,36 @@
         def _(k):
             w = other_w(k)
             pltpu.make_async_remote_copy(
-                src_ref=source.at[c, w, p], dst_ref=target.at[c, my_w, p],
+                src_ref=source.at[c, p, :, w], dst_ref=target.at[c, p, :, my_w],
                 send_sem=send_sem.at[c, g], recv_sem=recv_sem.at[c, g],
                 device_id=w_device(w), device_id_type=MESH,
             ).start()
 
-        target[c, my_w, p] = source[c, my_w, p]
+        for h in range(4):
+            target[c, p, h, my_w] = source[c, p, h, my_w]
 
     def wait_w(buffer, c, g, sem):
-        part = buffer.at[c, pl.ds(0, 31), 0]
+        part = buffer.at[c, 0, :, pl.ds(0, 31)]
         pltpu.make_async_copy(part, part, sem.at[c, g]).wait()
 
-    send_z(p_buf, q_buf, 0, 0, fz_s, fz_r)
-    send_z(p_buf, q_buf, 0, 1, fz_s, fz_r)
-
-    for c in range(2):
-        q_buf[c, my_p, my_h] = p_buf[c, my_p, my_h]
+    def rotate_bw(buffer, c, g, layer):
+        gates = [gate(layer, q) for q in BW_QUBITS]
+        p = 1 - my_p if g == 0 else my_p
+
+        @pl.loop(0, 4)
+        def _(h):
+            tiles = [buffer[c, p, h, w] for w in range(32)]
+            for bit in range(5):
+                tiles = rotate(tiles, bit, gates[bit])
+            for w in range(32):
+                buffer[c, p, h, w] = tiles[w]
+
+    for g in range(2):
+        send_z(p_buf, q_buf, 0, g, fz_s, fz_r)
+    q_buf[0, my_p, my_h] = p_buf[0, my_p, my_h]
+    for g in range(2):
+        rotate_bw(p_buf, 1, g, 0)
+        send_w(p_buf, q_buf, 1, g, fw_s, fw_r)
 
     square = (256, 256)
     rows = lax.broadcasted_iota(jnp.int32, square, 0)
@@ -168,7 +181,11 @@
                 a, b = to >> j & 1, of >> j & 1
                 entry = jnp.where(a == b, cosine, jnp.where(a == 1, sine, -sine))
                 matrix = entry if matrix is None else matrix * entry
-            gate_hi[layer, side], gate_lo[layer, side] = split(matrix)
+            high, low = split(matrix)
+            if side == 0:
+                gate_left[layer, :256], gate_left[layer, 256:] = high, low
+            else:
+                gate_right[layer, 0], gate_right[layer, 1] = high, low
 
     w_row, p_col = rows >> 3, cols >> 7
     fixed = ladder(my_w, 5) + ladder(my_z, 3) + (my_w >> 4 & my_z & 1)
@@ -181,36 +198,26 @@
         cz[0, h] = signs(with_h)
         cz[1, h] = signs(with_h + (rows >> 2 & 1) + (my_w & 1))
 
-    def rotate_bw(source, target, c, p, layer, forward):
-        gates = [gate(layer, q) for q in BW_QUBITS]
-
-        @pl.loop(0, 4)
-        def _(h):
-            tiles = [source[c, p, h, w] if forward else source[c, w, p, h] for w in range(32)]
-            for bit in range(5):
-                tiles = rotate(tiles, bit, gates[bit])
-            for w in range(32):
-                if forward:
-                    target[c, w, p, h] = tiles[w]
-                else:
-                    target[c, p, h, w] = tiles[w]
-
-    h_gates = [[gate(layer, q, (8, 256)) for q in (21, 22)] for layer in range(2)]
+    h_gates = [[gate(layer, q, (32, 256)) for q in (21, 22)] for layer in range(2)]
 
     def middle(c):
-        def both_sides(layer, block):
-            left = (gate_hi[layer, 0], gate_lo[layer, 0])
-            right = (gate_hi[layer, 1], gate_lo[layer, 1])
-            return dot3(split(dot3(left, split(block))), right)
-
-        @pl.loop(0, 4)
-        def _(h):
-            block = jnp.concatenate([w_buf[c, :, p, h].reshape(256, 128) for p in range(2)], axis=1)
-            ys[h] = both_sides(0, block)
-
-        @pl.loop(0, 32)
+        def left(layer, block):
+            high, low = split(block)
+            both = jnp.dot(gate_left[layer], high, preferred_element_type=F32)
+            return both[:256] + both[256:] + jnp.dot(gate_left[layer, :256], low, preferred_element_type=F32)
+
+        def right(layer, block):
+            high, low = split(block)
+            both = jnp.dot(jnp.concatenate([high, low], axis=0), gate_right[layer, 0], preferred_element_type=F32)
+            return both[:256] + both[256:] + jnp.dot(high, gate_right[layer, 1], preferred_element_type=F32)
+
+        for h in range(4):
+            block = jnp.concatenate([w_buf[c, p, h].reshape(256, 128) for p in range(2)], axis=1)
+            ys[h] = right(0, left(0, block))
+
+        @pl.loop(0, 8)
         def _(r):
-            part = pl.ds(pl.multiple_of(8 * r, 8), 8)
+            part = pl.ds(pl.multiple_of(32 * r, 32), 32)
             tiles = [ys[h, part] for h in range(4)]
             for layer in range(2):
                 for bit in range(2):
@@ -220,31 +227,16 @@
             for h in range(4):
                 ys[h, part] = tiles[h]
 
-        @pl.loop(0, 4)
-        def _(h):
-            block = both_sides(1, ys[h])
+        for h in range(4):
+            block = right(1, left(1, ys[h]))
             for p in range(2):
-                m_buf[c, :, p, h] = block[:, 128 * p:128 * p + 128].reshape(32, 8, 128)
-
-    def forward_z(c, g):
-        wait_z(q_buf, c, g, fz_r)
-        if c == 0:
-            send_z(p_buf, q_buf, 1, g, fz_s, fz_r)
-        rotate_bw(q_buf, q2, c, 1 - my_p if g == 0 else my_p, 0, True)
-        send_w(q2, w_buf, c, g, fw_s, fw_r)
-
-    def forward_w(c):
-        for g in range(2):
-            wait_w(w_buf, c, g, fw_r)
-        middle(c)
-        for g in range(2):
-            send_w(m_buf, v_buf, c, g, bw_s, bw_r)
-
-    def backward_w(c, g):
+                m_buf[c, p, h] = block[:, 128 * p:128 * p + 128].reshape(32, 8, 128)
+
+    def back(c, g):
         wait_w(v_buf, c, g, bw_r)
-        rotate_bw(v_buf, v2, c, 1 - my_p if g == 0 else my_p, 1, False)
+        rotate_bw(v_buf, c, g, 1)
         if c == 0 or g == 0:
-            send_z(v2, t_buf, c, g, bz_s, bz_r)
+            send_z(v_buf, t_buf, c, g, bz_s, bz_r)
         else:
             for i in range(QUARTERS):
                 part = pl.ds(8 * i, 8)
@@ -253,23 +245,38 @@
                 def _(k):
                     h = lax.rem(my_h + k, 4)
                     pltpu.make_async_remote_copy(
-                        src_ref=v2.at[c, my_p, h, part], dst_ref=t_buf.at[c, my_p, my_h, part],
+                        src_ref=v_buf.at[c, my_p, h, part], dst_ref=t_buf.at[c, my_p, my_h, part],
                         send_sem=last_s.at[i], recv_sem=last_r.at[i],
                         device_id=z_device(2 * h + my_p), device_id_type=MESH,
                     ).start()
         if g == 1:
-            t_buf[c, my_p, my_h] = v2[c, my_p, my_h]
-
-    forward_z(0, 0)
-    forward_z(0, 1)
-    forward_w(0)
-    forward_z(1, 0)
-    backward_w(0, 0)
-    forward_z(1, 1)
-    backward_w(0, 1)
-    forward_w(1)
-    backward_w(1, 0)
-    backward_w(1, 1)
+            t_buf[c, my_p, my_h] = v_buf[c, my_p, my_h]
+
+    wait_z(q_buf, 0, 0, fz_r)
+    rotate_bw(q_buf, 0, 0, 0)
+    send_w(q_buf, w_buf, 0, 0, fw_s, fw_r)
+    wait_w(q_buf, 1, 0, fw_r)
+    send_z(q_buf, w_buf, 1, 0, fz_s, fz_r)
+    wait_z(q_buf, 0, 1, fz_r)
+    rotate_bw(q_buf, 0, 1, 0)
+    send_w(q_buf, w_buf, 0, 1, fw_s, fw_r)
+    wait_w(q_buf, 1, 1, fw_r)
+    send_z(q_buf, w_buf, 1, 1, fz_s, fz_r)
+    w_buf[1, my_p, my_h] = q_buf[1, my_p, my_h]
+    for g in range(2):
+        wait_w(w_buf, 0, g, fw_r)
+    middle(0)
+    for g in range(2):
+        send_w(m_buf, v_buf, 0, g, bw_s, bw_r)
+    back(0, 0)
+    for g in range(2):
+        wait_z(w_buf, 1, g, fz_r)
+    middle(1)
+    for g in range(2):
+        send_w(m_buf, v_buf, 1, g, bw_s, bw_r)
+    back(0, 1)
+    back(1, 0)
+    back(1, 1)
 
     second = [gate(1, q) for q in (10, 16, 17, 18)]
     sub = lax.broadcasted_iota(jnp.int32, (8, 128), 0)
@@ -292,49 +299,43 @@
                 c, z = j & 1, j >> 1
                 parity = ladder(bw, 5) + (c & bw & 1) + (bw >> 4 & z & 1) + (z >> 2 & core & 1)
                 parity = parity + (z & z >> 1 & 1) + (z >> 1 & z >> 2 & 1)
-                o_buf[z, bw, c] = tiles[j] * (tile_signs[c] * signs(parity))
-
-        store(i).start()
+                out[z, bw, c] = tiles[j] * (tile_signs[c] * signs(parity))
 
     for c in range(2):
         for g in range(2):
             wait_z(p_buf, c, g, fz_s)
-            wait_w(q2, c, g, fw_s)
+            wait_w(q_buf, c, g, fw_s)
             wait_w(m_buf, c, g, bw_s)
             if c == 0 or g == 0:
-                wait_z(v2, c, g, bz_s)
+                wait_z(v_buf, c, g, bz_s)
     for i in range(QUARTERS):
-        part = v2.at[1, 0, pl.ds(0, 3), pl.ds(8 * i, 8)]
+        part = v_buf.at[1, 0, pl.ds(0, 3), pl.ds(8 * i, 8)]
         pltpu.make_async_copy(part, part, last_s.at[i]).wait()
-        store(i).wait()
 
 
 def shards(state, angles):
     view = (8, 32, 2, 8, 128)
     by_z = (2, 2, 4, 32, 8, 128)
-    by_w = (2, 32, 2, 4, 8, 128)
     pairs = pltpu.SemaphoreType.DMA((2, 2))
     quarters = pltpu.SemaphoreType.DMA((QUARTERS,))
     out = pl.pallas_call(
         kernel,
         out_shape=jax.ShapeDtypeStruct(view, F32),
-        in_specs=[pl.BlockSpec(memory_space=pl.ANY), pl.BlockSpec(memory_space=pltpu.VMEM)],
-        out_specs=pl.BlockSpec(memory_space=pl.ANY),
+        in_specs=[pl.BlockSpec(memory_space=pltpu.HBM)] * 2,
+        out_specs=pl.BlockSpec(memory_space=pltpu.VMEM),
         scratch_shapes=[
-            pltpu.VMEM(view, F32),
-            pltpu.VMEM(by_z, F32), pltpu.VMEM(by_z, F32),
-            pltpu.VMEM(by_w, F32), pltpu.VMEM(by_w, F32), pltpu.VMEM(by_w, F32), pltpu.VMEM(by_w, F32),
-            pltpu.VMEM(by_z, F32), pltpu.VMEM(by_z, F32),
-            pltpu.VMEM(view, F32),
+            pltpu.VMEM(view, F32), pltpu.VMEM((2, 27), F32),
+            pltpu.VMEM(by_z, F32), pltpu.VMEM(by_z, F32), pltpu.VMEM(by_z, F32),
+            pltpu.VMEM(by_z, F32), pltpu.VMEM(by_z, F32), pltpu.VMEM(by_z, F32),
             pltpu.VMEM((4, 256, 256), F32),
             pltpu.VMEM((2, 4, 256, 256), F32),
-            pltpu.VMEM((2, 2, 256, 256), BF16), pltpu.VMEM((2, 2, 256, 256), BF16),
-            quarters, quarters,
+            pltpu.VMEM((2, 512, 256), BF16), pltpu.VMEM((2, 2, 256, 256), BF16),
+            quarters, pltpu.SemaphoreType.DMA,
             pairs, pairs, pairs, pairs, pairs, pairs, pairs, pairs,
             quarters, quarters,
         ],
         compiler_params=pltpu.CompilerParams(
-            collective_id=0, has_side_effects=True, vmem_limit_bytes=48 * 2**20
+            collective_id=0, has_side_effects=True, vmem_limit_bytes=50 * 2**20
         ),
     )(state.reshape(view), angles)
     return out.reshape(state.shape)

time: 124 us -> 108 us (0.87)
  Pallas kernels: 121 us -> 106 us
  local copies, waits for them, and re-layouts: 3.59 us -> 2 us
    pallas_call x1, Pallas kernels: 121 us -> 106 us  [shards(): pl.pallas_call(kernel, out_shape=jax.ShapeDtypeStruct(view, F32), in_spec...]
    unnamed x5 -> x3, local copies, waits for them, and re-layouts: 3.59 us -> 2 us
where the time goes in v2:
time: 108 us
  Pallas kernels  106 us (98%)
  local copies, waits for them, and re-layouts  2 us (2%)
    pallas_call x1, Pallas kernels, shards(): pl.pallas_call(kernel, out_shape=jax.ShapeDtypeStruct(view, F32), in_spec...  106 us

profile of v2, /device:TPU:1, one launch (start us, length us, event | category | flops | bytes accessed | tf_op | source)
XLA Modules:
  0.0 108.3 jit_solution(18331090173962976328)
XLA Ops:
  0.0 0.0 copy-start
  0.0 0.7 copy-done
  0.7 106.3 %shard_map.28 = f32[8,32,2,8,128]{4,3,2,1,0:T(8,128)S(1)} custom-call(f32[8,32,2,8,128]{4,3,2,1,0:T(8,128)} %bitcast.3, f32[2,27]{1,0:T(2,128)S(1)} %copy-done), custom_call_target="tpu_custom_call" | custom-call | tf_op jit(solution)/shard_map/pallas_call | solution.py:321
  107.0 1.3 %copy.4 = f32[1,1,524288]{2,1,0:T(1,128)} copy(f32[1,1,524288]{2,1,0:T(1,128)S(1)} %bitcast.2) | data formatting | bytes 4194304
Async XLA Ops:
  0.0 0.7 copy-start

commit v3 on v2

v3 whole, which is shorter than its diff:
```python
import jax
import jax.numpy as jnp
from jax import lax
from jax.experimental import pallas as pl
from jax.experimental.pallas import tpu as pltpu
from jax.sharding import PartitionSpec as P

MESH = pl.DeviceIdType.MESH
F32, BF16 = jnp.float32, jnp.bfloat16
W_QUBITS = (19, 23, 24, 25, 26)
BW_QUBITS = (11, 12, 13, 14, 15)
ROW_QUBITS = (7, 8, 9) + W_QUBITS
COL_QUBITS = (0, 1, 2, 3, 4, 5, 6, 20)
QUARTERS = 4


def rotate(tiles, bit, gate):
    cosine, sine = gate
    out = list(tiles)
    for i in range(len(tiles)):
        if not i >> bit & 1:
            j = i | 1 << bit
            out[i] = cosine * tiles[i] - sine * tiles[j]
            out[j] = sine * tiles[i] + cosine * tiles[j]
    return out


def ladder(values, nbits):
    total = values & values >> 1
    parity = total & 1
    for j in range(1, nbits - 1):
        parity = parity + (total >> j & 1)
    return parity


def signs(parity):
    return (1 - 2 * (parity & 1)).astype(F32)


def split(value):
    high = value.astype(BF16)
    return high, (value - high.astype(F32)).astype(BF16)


def dot3(a, b):
    return (
        jnp.dot(a[0], b[0], preferred_element_type=F32)
        + jnp.dot(a[0], b[1], preferred_element_type=F32)
        + jnp.dot(a[1], b[0], preferred_element_type=F32)
    )


def at_w(w):
    return lax.div(w, 16), lax.rem(lax.div(w, 4), 4), lax.rem(lax.div(w, 2), 2), lax.rem(w, 2)


def kernel(
    state, angles, out,
    x, turns, p_buf, q_buf, w_buf, m_buf, v_buf, t_buf, r_buf, fx_buf, fy_buf, bx_buf, by_buf, ys, cz,
    gate_left, gate_right, gate_lane,
    load_sem, turns_sem, z_s, z_r, half_s, half_r, last_s, last_r, fx_s, fx_r, fy_s, fy_r, fc_s, fc_r, bx_s, bx_r, by_s, by_r, bc_s, bc_r,
):
    grp, dev = lax.axis_index("grp"), lax.axis_index("dev")
    core, my_z, x_lo = lax.rem(dev, 2), lax.rem(lax.div(dev, 2), 8), lax.div(dev, 16)
    my_y, x_hi = lax.rem(grp, 4), lax.div(grp, 4)
    my_w = core + 2 * x_lo + 4 * grp
    my_p, my_h = lax.rem(my_z, 2), lax.div(my_z, 2)

    def z_device(z):
        return (grp, 16 * x_lo + 2 * z + core)

    def x_peer(k):
        there = lax.rem(2 * x_hi + x_lo + k, 4)
        return lax.div(there, 2), lax.rem(there, 2)

    def x_device(hi, lo):
        return (4 * hi + my_y, 16 * lo + 2 * my_z + core)

    def y_device(y):
        return (4 * x_hi + y, dev)

    core_device = (grp, dev + 1 - 2 * core)

    def load(i):
        part = pl.ds(8 * i, 8)
        return pltpu.make_async_copy(state.at[:, part], x.at[:, part], load_sem.at[i])

    load_turns = pltpu.make_async_copy(angles, turns, turns_sem)
    load_turns.start()
    for i in range(QUARTERS):
        load(i).start()
    barrier = pltpu.get_barrier_semaphore()

    @pl.loop(1, 8)
    def _(k):
        pl.semaphore_signal(barrier, inc=1, device_id=z_device(lax.rem(my_z + k, 8)), device_id_type=MESH)

    @pl.loop(1, 4)
    def _(k):
        pl.semaphore_signal(barrier, inc=1, device_id=x_device(*x_peer(k)), device_id_type=MESH)
        pl.semaphore_signal(barrier, inc=1, device_id=y_device(lax.rem(my_y + k, 4)), device_id_type=MESH)

    pl.semaphore_signal(barrier, inc=1, device_id=core_device, device_id_type=MESH)

    load_turns.wait()
    half = 0.5 * turns[...]
    cosines, sines = jnp.cos(half), jnp.sin(half)

    def gate(layer, qubit, shape=(8, 128)):
        at = (slice(layer, layer + 1), slice(qubit, qubit + 1))
        return jnp.broadcast_to(cosines[at], shape), jnp.broadcast_to(sines[at], shape)

    first = [gate(0, q) for q in (10, 16, 17, 18)]
    for i in range(QUARTERS):
        load(i).wait()

        @pl.loop(8 * i, 8 * i + 8)
        def _(bw):
            tiles = [x[j >> 1, bw, j & 1] for j in range(16)]
            place = at_w(bw)
            for bit in range(4):
                tiles = rotate(tiles, bit, first[bit])
            for j in range(16):
                z = j >> 1
                p_buf[(j & 1, z & 1, z >> 1) + place] = tiles[j]

    pl.semaphore_wait(barrier, 14)

    def parity(g):
        return 1 - my_p if g == 0 else my_p

    def to_z(source, target, place, h, p, send_sem, recv_sem):
        pltpu.make_async_remote_copy(
            src_ref=source.at[(place[0], p, h) + place[1:]], dst_ref=target.at[(place[0], my_p, my_h) + place[1:]],
            send_sem=send_sem, recv_sem=recv_sem, device_id=z_device(2 * h + p), device_id_type=MESH,
        ).start()

    def send_z(source, target, place, g, send_sem, recv_sem):
        if g == 0:
            @pl.loop(0, 4)
            def _(h):
                to_z(source, target, place, h, 1 - my_p, send_sem, recv_sem)
        else:
            @pl.loop(0, 3)
            def _(k):
                to_z(source, target, place, k + lax.div(k + 4 - my_h, 4), my_p, send_sem, recv_sem)

    def wait_z(buffer, place, g, sem):
        part = buffer.at[(place[0], 0, pl.ds(0, 4 - g)) + place[1:]]
        pltpu.make_async_copy(part, part, sem).wait()

    def send_x(source, target, c, g, send_sem, recv_sem):
        p = parity(g)

        @pl.loop(1, 4)
        def _(k):
            hi, lo = x_peer(k)
            pltpu.make_async_remote_copy(
                src_ref=source.at[c, p, :, hi, :, lo], dst_ref=target.at[c, p, :, x_hi, :, x_lo],
                send_sem=send_sem.at[c, g], recv_sem=recv_sem.at[c, g],
                device_id=x_device(hi, lo), device_id_type=MESH,
            ).start()

        target[c, p, :, x_hi, :, x_lo] = source[c, p, :, x_hi, :, x_lo]

    def send_y(source, target, c, g, send_sem, recv_sem):
        p = parity(g)

        @pl.loop(1, 4)
        def _(k):
            y = lax.rem(my_y + k, 4)
            pltpu.make_async_remote_copy(
                src_ref=source.at[c, p, :, :, y], dst_ref=target.at[c, p, :, :, my_y],
                send_sem=send_sem.at[c, g], recv_sem=recv_sem.at[c, g],
                device_id=y_device(y), device_id_type=MESH,
            ).start()

        target[c, p, :, :, my_y] = source[c, p, :, :, my_y]

    def send_core(source, target, c, g, send_sem, recv_sem):
        p = parity(g)
        pltpu.make_async_remote_copy(
            src_ref=source.at[c, p, :, :, :, :, 1 - core], dst_ref=target.at[c, p, :, :, :, :, core],
            send_sem=send_sem.at[c, g], recv_sem=recv_sem.at[c, g],
            device_id=core_device, device_id_type=MESH,
        ).start()
        target[c, p, :, :, :, :, core] = source[c, p, :, :, :, :, core]

    def wait_w(c, g, sem, n=3):
        part = t_buf.at[0, 0, pl.ds(0, n)]
        pltpu.make_async_copy(part, part, sem.at[c, g]).wait()

    def hop(n, source, target, c, g, sems):
        if (n + g) % 2 == 0:
            send_x(source, target, c, g, sems[0], sems[1])
        else:
            send_y(source, target, c, g, sems[2], sems[3])

    def wait_hop(n, c, g, sems):
        wait_w(c, g, sems[1] if (n + g) % 2 == 0 else sems[3])

    forth, home = (fx_s, fx_r, fy_s, fy_r), (bx_s, bx_r, by_s, by_r)

    def rotate_bw(buffer, c, g, layer):
        gates = [gate(layer, q) for q in BW_QUBITS]
        p = parity(g)

        @pl.loop(0, 4)
        def _(h):
            spots = [(c, p, h, w >> 4, w >> 2 & 3, w >> 1 & 1, w & 1) for w in range(32)]
            tiles = [buffer[spot] for spot in spots]
            for bit in range(5):
                tiles = rotate(tiles, bit, gates[bit])
            for spot, tile in zip(spots, tiles):
                buffer[spot] = tile

    for g in range(2):
        send_z(p_buf, q_buf, (0,), g, z_s.at[g], z_r.at[g])
    for g in range(2):
        rotate_bw(p_buf, 1, g, 0)
        hop(0, p_buf, fx_buf, 1, g, forth)
    q_buf[0, my_p, my_h] = p_buf[0, my_p, my_h]

    square = (256, 256)
    rows = lax.broadcasted_iota(jnp.int32, square, 0)
    cols = lax.broadcasted_iota(jnp.int32, square, 1)
    for layer in range(2):
        for side, qubits in enumerate((ROW_QUBITS, COL_QUBITS)):
            matrix = None
            for j, q in enumerate(qubits):
                cosine, sine = gate(layer, q, square)
                to, of = (rows, cols) if side == 0 else (cols, rows)
                a, b = to >> j & 1, of >> j & 1
                entry = jnp.where(a == b, cosine, jnp.where(a == 1, sine, -sine))
                lanes = jnp.where(a == b, matrix, 0.0) if j == 7 else None
                matrix = entry if matrix is None else matrix * entry
            high, low = split(matrix)
            if side == 0:
                gate_left[layer, :256], gate_left[layer, 256:] = high, low
            else:
                gate_right[layer, 0], gate_right[layer, 1] = high, low
                gate_lane[layer, 0], gate_lane[layer, 1] = split(lanes)

    w_row, p_col = rows >> 3, cols >> 7
    fixed = ladder(my_w, 5) + ladder(my_z, 3) + (my_w >> 4 & my_z & 1)
    cross = (
        ladder(cols & 127, 7) + (cols >> 6 & rows & 1) + ladder(rows & 7, 3) + (my_z >> 2 & w_row & 1)
        + (w_row & p_col & 1) + ladder(w_row >> 1, 4) + fixed
    )
    for h in range(4):
        with_h = cross + (p_col & h & 1) + (h >> 1 & w_row >> 1 & 1) + (h & h >> 1 & 1)
        cz[0, h] = signs(with_h)
        cz[1, h] = signs(with_h + (rows >> 2 & 1) + (my_w & 1))

    h_gates = [[gate(layer, q, (32, 256)) for q in (21, 22)] for layer in range(2)]

    def left(layer, block):
        high, low = split(block)
        both = jnp.dot(gate_left[layer], high, preferred_element_type=F32)
        return both[:256] + both[256:] + jnp.dot(gate_left[layer, :256], low, preferred_element_type=F32)

    def right(gates, layer, block):
        high, low = split(block)
        both = jnp.dot(jnp.concatenate([high, low], axis=0), gates[layer, 0], preferred_element_type=F32)
        return both[:256] + both[256:] + jnp.dot(high, gates[layer, 1], preferred_element_type=F32)

    def rows_and_lanes(buffer, g, layer):
        p = parity(g)
        for h in (0, 2):
            block = jnp.concatenate([buffer[1, p, h + i].reshape(256, 128) for i in range(2)], axis=1)
            block = right(gate_lane, layer, left(layer, block))
            for i in range(2):
                buffer[1, p, h + i] = block[:, 128 * i:128 * i + 128].reshape(2, 4, 2, 2, 8, 128)

    z_gates = [[gate(layer, q) for q in (20, 21, 22)] for layer in range(2)]

    def middle_z(half):
        @pl.loop(0, 16)
        def _(k):
            w = 16 * half + k
            place = at_w(w)
            tiles = [w_buf[(1, z & 1, z >> 1) + place] for z in range(8)]
            for bit in range(3):
                tiles = rotate(tiles, bit, z_gates[0][bit])
            part = pl.ds(pl.multiple_of(8 * w, 8), 8)
            for z in range(8):
                tiles[z] = tiles[z] * cz[1, z >> 1, part, 128 * (z & 1):128 * (z & 1) + 128]
            for bit in range(3):
                tiles = rotate(tiles, bit, z_gates[1][bit])
            for z in range(8):
                m_buf[(1, z & 1, z >> 1) + place] = tiles[z]

    def middle(c):
        for h in range(4):
            block = jnp.concatenate([w_buf[c, p, h].reshape(256, 128) for p in range(2)], axis=1)
            ys[h] = right(gate_right, 0, left(0, block))

        @pl.loop(0, 8)
        def _(r):
            part = pl.ds(pl.multiple_of(32 * r, 32), 32)
            tiles = [ys[h, part] for h in range(4)]
            for layer in range(2):
                for bit in range(2):
                    tiles = rotate(tiles, bit, h_gates[layer][bit])
                if layer == 0:
                    tiles = [tiles[h] * cz[c, h, part] for h in range(4)]
            for h in range(4):
                ys[h, part] = tiles[h]

        for h in range(4):
            block = right(gate_right, 1, left(1, ys[h]))
            for p in range(2):
                m_buf[c, p, h] = block[:, 128 * p:128 * p + 128].reshape(2, 4, 2, 2, 8, 128)

    def forward_1(g):
        wait_w(1, g, fc_r, 2)
        rows_and_lanes(q_buf, g, 0)

    def back_0(g):
        wait_w(0, g, bc_r, 2)
        rotate_bw(v_buf, 0, g, 1)
        if g == 0:
            send_z(v_buf, t_buf, (0,), 0, z_s.at[2], z_r.at[2])
            return

        @pl.loop(0, 3)
        def _(k):
            h = k + lax.div(k + 4 - my_h, 4)
            for i in range(QUARTERS):
                to_z(v_buf, t_buf, (0, i >> 1, pl.ds(2 * (i & 1), 2)), h, my_p, last_s.at[i], last_r.at[i])

        t_buf[0, my_p, my_h] = v_buf[0, my_p, my_h]

    for g in range(2):
        wait_hop(0, 1, g, forth)
        hop(1, fx_buf, fy_buf, 1, g, forth)
    for g in range(2):
        wait_hop(1, 1, g, forth)
        send_core(fy_buf, q_buf, 1, g, fc_s, fc_r)
    for g in range(2):
        forward_1(g)
    for half in range(2):
        for g in range(2):
            send_z(q_buf, w_buf, (1, half), g, half_s.at[0, half, g], half_r.at[0, half, g])
    w_buf[1, my_p, my_h] = q_buf[1, my_p, my_h]
    for g in range(2):
        wait_z(q_buf, (0,), g, z_r.at[g])
        rotate_bw(q_buf, 0, g, 0)
        hop(0, q_buf, fx_buf, 0, g, forth)
    for g in range(2):
        wait_hop(0, 0, g, forth)
        hop(1, fx_buf, fy_buf, 0, g, forth)

    def turn_1(half):
        for g in range(2):
            wait_z(w_buf, (1, half), g, half_r.at[0, half, g])
        middle_z(half)
        for g in range(2):
            send_z(m_buf, r_buf, (1, half), g, half_s.at[1, half, g], half_r.at[1, half, g])

    turn_1(0)
    for g in range(2):
        wait_hop(1, 0, g, forth)
        send_core(fy_buf, w_buf, 0, g, fc_s, fc_r)
    for g in range(2):
        wait_w(0, g, fc_r, 2)
    middle(0)
    for g in range(2):
        hop(0, m_buf, bx_buf, 0, g, home)
    turn_1(1)
    r_buf[1, my_p, my_h] = m_buf[1, my_p, my_h]
    for g in range(2):
        wait_hop(0, 0, g, home)
        hop(1, bx_buf, by_buf, 0, g, home)
    for g in range(2):
        wait_hop(1, 0, g, home)
        send_core(by_buf, v_buf, 0, g, bc_s, bc_r)
    for g in range(2):
        back_0(g)
    for half in range(2):
        for g in range(2):
            wait_z(r_buf, (1, half), g, half_r.at[1, half, g])
    for g in range(2):
        rows_and_lanes(r_buf, g, 1)
        hop(0, r_buf, bx_buf, 1, g, home)
    for g in range(2):
        wait_hop(0, 1, g, home)
        hop(1, bx_buf, by_buf, 1, g, home)
    for g in range(2):
        wait_hop(1, 1, g, home)
        send_core(by_buf, t_buf, 1, g, bc_s, bc_r)
    for g in range(2):
        wait_w(1, g, bc_r, 2)
        rotate_bw(t_buf, 1, g, 1)

    second = [gate(1, q) for q in (10, 16, 17, 18)]
    sub = lax.broadcasted_iota(jnp.int32, (8, 128), 0)
    lane = lax.broadcasted_iota(jnp.int32, (8, 128), 1)
    base = ladder(lane, 7) + (lane >> 6 & sub & 1) + ladder(sub, 3)
    base = base + ladder(dev, 5) + ladder(grp, 3) + (dev >> 4 & grp & 1)
    tile_signs = [signs(base + c * (sub >> 2 & 1)) for c in range(2)]
    wait_z(t_buf, (0,), 0, z_r.at[2])
    for i in range(QUARTERS):
        wait_z(t_buf, (0, i >> 1, pl.ds(2 * (i & 1), 2)), 1, last_r.at[i])

        @pl.loop(8 * i, 8 * i + 8)
        def _(bw):
            place = at_w(bw)
            tiles = [t_buf[(j & 1, j >> 1 & 1, j >> 2) + place] for j in range(16)]
            for bit in range(4):
                tiles = rotate(tiles, bit, second[bit])
            for j in range(16):
                c, z = j & 1, j >> 1
                odd = ladder(bw, 5) + (c & bw & 1) + (bw >> 4 & z & 1) + (z >> 2 & core & 1)
                odd = odd + (z & z >> 1 & 1) + (z >> 1 & z >> 2 & 1)
                out[z, bw, c] = tiles[j] * (tile_signs[c] * signs(odd))

    for g in range(2):
        wait_z(p_buf, (0,), g, z_s.at[g])
        for half in range(2):
            for way in range(2):
                wait_z(r_buf, (1, half), g, half_s.at[way, half, g])
        for c in range(2):
            for sem, n in ((fx_s, 3), (fy_s, 3), (fc_s, 2), (bx_s, 3), (by_s, 3), (bc_s, 2)):
                wait_w(c, g, sem, n)
    wait_z(v_buf, (0,), 0, z_s.at[2])
    for i in range(QUARTERS):
        wait_z(v_buf, (0, i >> 1, pl.ds(2 * (i & 1), 2)), 1, last_s.at[i])


def shards(state, angles):
    view = (8, 32, 2, 8, 128)
    by_z = (2, 2, 4, 2, 4, 2, 2, 8, 128)
    pairs = pltpu.SemaphoreType.DMA((2, 2))
    quarters = pltpu.SemaphoreType.DMA((QUARTERS,))
    out = pl.pallas_call(
        kernel,
        out_shape=jax.ShapeDtypeStruct(view, F32),
        in_specs=[pl.BlockSpec(memory_space=pltpu.HBM)] * 2,
        out_specs=pl.BlockSpec(memory_space=pltpu.VMEM),
        scratch_shapes=[
            pltpu.VMEM(view, F32), pltpu.VMEM((2, 27), F32),
            *[pltpu.VMEM(by_z, F32)] * 11,
            pltpu.VMEM((4, 256, 256), F32),
            pltpu.VMEM((2, 4, 256, 256), F32),
            pltpu.VMEM((2, 512, 256), BF16), pltpu.VMEM((2, 2, 256, 256), BF16), pltpu.VMEM((2, 2, 256, 256), BF16),
            quarters, pltpu.SemaphoreType.DMA,
            pltpu.SemaphoreType.DMA((3,)), pltpu.SemaphoreType.DMA((3,)),
            pltpu.SemaphoreType.DMA((2, 2, 2)), pltpu.SemaphoreType.DMA((2, 2, 2)),
            quarters, quarters,
            *[pairs] * 12,
        ],
        compiler_params=pltpu.CompilerParams(
            collective_id=0, has_side_effects=True, vmem_limit_bytes=50 * 2**20
        ),
    )(state.reshape(view), angles)
    return out.reshape(state.shape)


def solution(mesh):
    placed = (P("grp", "dev", None), P())
    return jax.shard_map(
        shards, mesh=mesh, in_specs=placed, out_specs=P("grp", "dev", None), check_vma=False
    )
```

time: 108 us -> 105 us (0.972)
  Pallas kernels: 106 us -> 103 us
    pallas_call x1, Pallas kernels: 106 us -> 103 us  [shards(): pl.pallas_call(kernel, out_shape=jax.ShapeDtypeStruct(view, F32), in_spec...]
where the time goes in v3:
time: 105 us
  Pallas kernels  103 us (98%)
  local copies, waits for them, and re-layouts  2 us (2%)
    pallas_call x1, Pallas kernels, shards(): pl.pallas_call(kernel, out_shape=jax.ShapeDtypeStruct(view, F32), in_spec...  103 us

profile of v3, /device:TPU:1, one launch (start us, length us, event | category | flops | bytes accessed | tf_op | source)
XLA Modules:
  0.0 104.8 jit_solution(11479537868883883650)
XLA Ops:
  0.0 0.0 copy-start
  0.0 0.7 copy-done
  0.7 102.8 %shard_map.28 = f32[8,32,2,8,128]{4,3,2,1,0:T(8,128)S(1)} custom-call(f32[8,32,2,8,128]{4,3,2,1,0:T(8,128)} %bitcast.3, f32[2,27]{1,0:T(2,128)S(1)} %copy-done), custom_call_target="tpu_custom_call" | custom-call | tf_op jit(solution)/shard_map/pallas_call | solution.py:436
  103.5 1.3 %copy.4 = f32[1,1,524288]{2,1,0:T(1,128)} copy(f32[1,1,524288]{2,1,0:T(1,128)S(1)} %bitcast.2) | data formatting | bytes 4194304
Async XLA Ops:
  0.0 0.7 copy-start

commit v4 on v3

--- a/solution.py
+++ b/solution.py
@@ -111,6 +111,97 @@
         return jnp.broadcast_to(cosines[at], shape), jnp.broadcast_to(sines[at], shape)
 
     first = [gate(0, q) for q in (10, 16, 17, 18)]
+    def quarter(i):
+        return i >> 1, pl.ds(2 * (i & 1), 2)
+
+    def parity(g):
+        return 1 - my_p if g == 0 else my_p
+
+    def to_z(source, target, place, h, p, send_sem, recv_sem):
+        pltpu.make_async_remote_copy(
+            src_ref=source.at[(place[0], p, h) + place[1:]], dst_ref=target.at[(place[0], my_p, my_h) + place[1:]],
+            send_sem=send_sem, recv_sem=recv_sem, device_id=z_device(2 * h + p), device_id_type=MESH,
+        ).start()
+
+    def send_z(source, target, place, g, send_sem, recv_sem):
+        if g == 0:
+            @pl.loop(0, 4)
+            def _(h):
+                to_z(source, target, place, h, 1 - my_p, send_sem, recv_sem)
+        else:
+            @pl.loop(0, 3)
+            def _(k):
+                to_z(source, target, place, k + lax.div(k + 4 - my_h, 4), my_p, send_sem, recv_sem)
+
+    def wait_z(buffer, place, g, sem):
+        part = buffer.at[(place[0], 0, pl.ds(0, 4 - g)) + place[1:]]
+        pltpu.make_async_copy(part, part, sem).wait()
+
+    def send_x(source, target, c, g, send_sem, recv_sem):
+        p = parity(g)
+
+        @pl.loop(1, 4)
+        def _(k):
+            hi, lo = x_peer(k)
+            pltpu.make_async_remote_copy(
+                src_ref=source.at[c, p, :, hi, :, lo], dst_ref=target.at[c, p, :, x_hi, :, x_lo],
+                send_sem=send_sem.at[c, g], recv_sem=recv_sem.at[c, g],
+                device_id=x_device(hi, lo), device_id_type=MESH,
+            ).start()
+
+        target[c, p, :, x_hi, :, x_lo] = source[c, p, :, x_hi, :, x_lo]
+
+    def send_y(source, target, c, g, send_sem, recv_sem):
+        p = parity(g)
+
+        @pl.loop(1, 4)
+        def _(k):
+            y = lax.rem(my_y + k, 4)
+            pltpu.make_async_remote_copy(
+                src_ref=source.at[c, p, :, :, y], dst_ref=target.at[c, p, :, :, my_y],
+                send_sem=send_sem.at[c, g], recv_sem=recv_sem.at[c, g],
+                device_id=y_device(y), device_id_type=MESH,
+            ).start()
+
+        target[c, p, :, :, my_y] = source[c, p, :, :, my_y]
+
+    def send_core(source, target, c, g, send_sem, recv_sem):
+        p = parity(g)
+        pltpu.make_async_remote_copy(
+            src_ref=source.at[c, p, :, :, :, :, 1 - core], dst_ref=target.at[c, p, :, :, :, :, core],
+            send_sem=send_sem.at[c, g], recv_sem=recv_sem.at[c, g],
+            device_id=core_device, device_id_type=MESH,
+        ).start()
+        target[c, p, :, :, :, :, core] = source[c, p, :, :, :, :, core]
+
+    def wait_w(c, g, sem, n=3):
+        part = t_buf.at[0, 0, pl.ds(0, n)]
+        pltpu.make_async_copy(part, part, sem.at[c, g]).wait()
+
+    def hop(n, source, target, c, g, sems):
+        if (n + g) % 2 == 0:
+            send_x(source, target, c, g, sems[0], sems[1])
+        else:
+            send_y(source, target, c, g, sems[2], sems[3])
+
+    def wait_hop(n, c, g, sems):
+        wait_w(c, g, sems[1] if (n + g) % 2 == 0 else sems[3])
+
+    forth, home = (fx_s, fx_r, fy_s, fy_r), (bx_s, bx_r, by_s, by_r)
+
+    def rotate_bw(buffer, c, g, layer):
+        gates = [gate(layer, q) for q in BW_QUBITS]
+        p = parity(g)
+
+        @pl.loop(0, 4)
+        def _(h):
+            spots = [(c, p, h, w >> 4, w >> 2 & 3, w >> 1 & 1, w & 1) for w in range(32)]
+            tiles = [buffer[spot] for spot in spots]
+            for bit in range(5):
+                tiles = rotate(tiles, bit, gates[bit])
+            for spot, tile in zip(spots, tiles):
+                buffer[spot] = tile
+
     for i in range(QUARTERS):
         load(i).wait()
 
@@ -124,98 +215,11 @@
                 z = j >> 1
                 p_buf[(j & 1, z & 1, z >> 1) + place] = tiles[j]
 
-    pl.semaphore_wait(barrier, 14)
-
-    def parity(g):
-        return 1 - my_p if g == 0 else my_p
-
-    def to_z(source, target, place, h, p, send_sem, recv_sem):
-        pltpu.make_async_remote_copy(
-            src_ref=source.at[(place[0], p, h) + place[1:]], dst_ref=target.at[(place[0], my_p, my_h) + place[1:]],
-            send_sem=send_sem, recv_sem=recv_sem, device_id=z_device(2 * h + p), device_id_type=MESH,
-        ).start()
-
-    def send_z(source, target, place, g, send_sem, recv_sem):
-        if g == 0:
-            @pl.loop(0, 4)
-            def _(h):
-                to_z(source, target, place, h, 1 - my_p, send_sem, recv_sem)
-        else:
-            @pl.loop(0, 3)
-            def _(k):
-                to_z(source, target, place, k + lax.div(k + 4 - my_h, 4), my_p, send_sem, recv_sem)
-
-    def wait_z(buffer, place, g, sem):
-        part = buffer.at[(place[0], 0, pl.ds(0, 4 - g)) + place[1:]]
-        pltpu.make_async_copy(part, part, sem).wait()
-
-    def send_x(source, target, c, g, send_sem, recv_sem):
-        p = parity(g)
-
-        @pl.loop(1, 4)
-        def _(k):
-            hi, lo = x_peer(k)
-            pltpu.make_async_remote_copy(
-                src_ref=source.at[c, p, :, hi, :, lo], dst_ref=target.at[c, p, :, x_hi, :, x_lo],
-                send_sem=send_sem.at[c, g], recv_sem=recv_sem.at[c, g],
-                device_id=x_device(hi, lo), device_id_type=MESH,
-            ).start()
-
-        target[c, p, :, x_hi, :, x_lo] = source[c, p, :, x_hi, :, x_lo]
-
-    def send_y(source, target, c, g, send_sem, recv_sem):
-        p = parity(g)
-
-        @pl.loop(1, 4)
-        def _(k):
-            y = lax.rem(my_y + k, 4)
-            pltpu.make_async_remote_copy(
-                src_ref=source.at[c, p, :, :, y], dst_ref=target.at[c, p, :, :, my_y],
-                send_sem=send_sem.at[c, g], recv_sem=recv_sem.at[c, g],
-                device_id=y_device(y), device_id_type=MESH,
-            ).start()
-
-        target[c, p, :, :, my_y] = source[c, p, :, :, my_y]
-
-    def send_core(source, target, c, g, send_sem, recv_sem):
-        p = parity(g)
-        pltpu.make_async_remote_copy(
-            src_ref=source.at[c, p, :, :, :, :, 1 - core], dst_ref=target.at[c, p, :, :, :, :, core],
-            send_sem=send_sem.at[c, g], recv_sem=recv_sem.at[c, g],
-            device_id=core_device, device_id_type=MESH,
-        ).start()
-        target[c, p, :, :, :, :, core] = source[c, p, :, :, :, :, core]
-
-    def wait_w(c, g, sem, n=3):
-        part = t_buf.at[0, 0, pl.ds(0, n)]
-        pltpu.make_async_copy(part, part, sem.at[c, g]).wait()
-
-    def hop(n, source, target, c, g, sems):
-        if (n + g) % 2 == 0:
-            send_x(source, target, c, g, sems[0], sems[1])
-        else:
-            send_y(source, target, c, g, sems[2], sems[3])
-
-    def wait_hop(n, c, g, sems):
-        wait_w(c, g, sems[1] if (n + g) % 2 == 0 else sems[3])
-
-    forth, home = (fx_s, fx_r, fy_s, fy_r), (bx_s, bx_r, by_s, by_r)
-
-    def rotate_bw(buffer, c, g, layer):
-        gates = [gate(layer, q) for q in BW_QUBITS]
-        p = parity(g)
-
-        @pl.loop(0, 4)
-        def _(h):
-            spots = [(c, p, h, w >> 4, w >> 2 & 3, w >> 1 & 1, w & 1) for w in range(32)]
-            tiles = [buffer[spot] for spot in spots]
-            for bit in range(5):
-                tiles = rotate(tiles, bit, gates[bit])
-            for spot, tile in zip(spots, tiles):
-                buffer[spot] = tile
-
-    for g in range(2):
-        send_z(p_buf, q_buf, (0,), g, z_s.at[g], z_r.at[g])
+        if i == 0:
+            pl.semaphore_wait(barrier, 14)
+        for g in range(2):
+            send_z(p_buf, q_buf, (0,) + quarter(i), g, z_s.at[g], z_r.at[g])
+
     for g in range(2):
         rotate_bw(p_buf, 1, g, 0)
         hop(0, p_buf, fx_buf, 1, g, forth)
@@ -327,7 +331,7 @@
         def _(k):
             h = k + lax.div(k + 4 - my_h, 4)
             for i in range(QUARTERS):
-                to_z(v_buf, t_buf, (0, i >> 1, pl.ds(2 * (i & 1), 2)), h, my_p, last_s.at[i], last_r.at[i])
+                to_z(v_buf, t_buf, (0,) + quarter(i), h, my_p, last_s.at[i], last_r.at[i])
 
         t_buf[0, my_p, my_h] = v_buf[0, my_p, my_h]
 
@@ -401,7 +405,7 @@
     tile_signs = [signs(base + c * (sub >> 2 & 1)) for c in range(2)]
     wait_z(t_buf, (0,), 0, z_r.at[2])
     for i in range(QUARTERS):
-        wait_z(t_buf, (0, i >> 1, pl.ds(2 * (i & 1), 2)), 1, last_r.at[i])
+        wait_z(t_buf, (0,) + quarter(i), 1, last_r.at[i])
 
         @pl.loop(8 * i, 8 * i + 8)
         def _(bw):
@@ -425,7 +429,7 @@
                 wait_w(c, g, sem, n)
     wait_z(v_buf, (0,), 0, z_s.at[2])
     for i in range(QUARTERS):
-        wait_z(v_buf, (0, i >> 1, pl.ds(2 * (i & 1), 2)), 1, last_s.at[i])
+        wait_z(v_buf, (0,) + quarter(i), 1, last_s.at[i])
 
 
 def shards(state, angles):

time: 105 us -> 104 us (level)
  no operation moved by 1% of the time
where the time goes in v4:
time: 104 us
  Pallas kernels  102 us (98%)
  local copies, waits for them, and re-layouts  2 us (2%)
    pallas_call x1, Pallas kernels, shards(): pl.pallas_call(kernel, out_shape=jax.ShapeDtypeStruct(view, F32), in_spec...  102 us

profile of v4, /device:TPU:1, one launch (start us, length us, event | category | flops | bytes accessed | tf_op | source)
XLA Modules:
  0.0 103.8 jit_solution(12791811112321977846)
XLA Ops:
  0.0 0.0 copy-start
  0.0 0.7 copy-done
  0.7 101.8 %shard_map.28 = f32[8,32,2,8,128]{4,3,2,1,0:T(8,128)S(1)} custom-call(f32[8,32,2,8,128]{4,3,2,1,0:T(8,128)} %bitcast.3, f32[2,27]{1,0:T(2,128)S(1)} %copy-done), custom_call_target="tpu_custom_call" | custom-call | tf_op jit(solution)/shard_map/pallas_call | solution.py:440
  102.5 1.3 %copy.4 = f32[1,1,524288]{2,1,0:T(1,128)} copy(f32[1,1,524288]{2,1,0:T(1,128)S(1)} %bitcast.2) | data formatting | bytes 4194304
Async XLA Ops:
  0.0 0.7 copy-start

commit v5 on v4

--- a/solution.py
+++ b/solution.py
@@ -327,12 +327,8 @@
             send_z(v_buf, t_buf, (0,), 0, z_s.at[2], z_r.at[2])
             return
 
-        @pl.loop(0, 3)
-        def _(k):
-            h = k + lax.div(k + 4 - my_h, 4)
-            for i in range(QUARTERS):
-                to_z(v_buf, t_buf, (0,) + quarter(i), h, my_p, last_s.at[i], last_r.at[i])
-
+        for i in range(QUARTERS):
+            send_z(v_buf, t_buf, (0,) + quarter(i), 1, last_s.at[i], last_r.at[i])
         t_buf[0, my_p, my_h] = v_buf[0, my_p, my_h]
 
     for g in range(2):

time: 104 us -> 104 us (level)
  no operation moved by 1% of the time
where the time goes in v5:
time: 104 us
  Pallas kernels  102 us (98%)
  local copies, waits for them, and re-layouts  2 us (2%)
    pallas_call x1, Pallas kernels, shards(): pl.pallas_call(kernel, out_shape=jax.ShapeDtypeStruct(view, F32), in_spec...  102 us

profile of v5, /device:TPU:1, one launch (start us, length us, event | category | flops | bytes accessed | tf_op | source)
XLA Modules:
  0.0 103.8 jit_solution(5403128826010588641)
XLA Ops:
  0.0 0.0 copy-start
  0.0 0.7 copy-done
  0.7 101.8 %shard_map.28 = f32[8,32,2,8,128]{4,3,2,1,0:T(8,128)S(1)} custom-call(f32[8,32,2,8,128]{4,3,2,1,0:T(8,128)} %bitcast.3, f32[2,27]{1,0:T(2,128)S(1)} %copy-done), custom_call_target="tpu_custom_call" | custom-call | tf_op jit(solution)/shard_map/pallas_call | solution.py:436
  102.5 1.3 %copy.4 = f32[1,1,524288]{2,1,0:T(1,128)} copy(f32[1,1,524288]{2,1,0:T(1,128)S(1)} %bitcast.2) | data formatting | bytes 4194304
Async XLA Ops:
  0.0 0.7 copy-start
